TPU v7x, 512 devices: a whole 4x4x16 slice. The times are simulated.
512 devices in a mesh: exp: 64 (over x, z), ctx: 8 (over y, core).
Axes of the slice: x: 4, y: 4, z: 16, core: 2. Of those that a mesh axis runs over, the one named last changes fastest.
Arguments:
- y_first: bfloat16 [8192, 1024], P('exp', 'ctx'), may hold values from -6 to 6
- y_second: bfloat16 [8192, 1024], P('exp', 'ctx'), may hold values from -6 to 6
- grad_first: bfloat16 [8192, 1024], P('exp', 'ctx'), may hold values from -6 to 6
- grad_second: bfloat16 [8192, 1024], P('exp', 'ctx'), may hold values from -6 to 6
- expert_ids: int32 [8192, 6], P('exp'), may hold values from 0 to 63, all different within a row; in each aligned block of 128 rows (0 to 127, 128 to 255, ...) at most 16 rows name the same one
- gate_fixed: int32 [8192, 6], P('exp'), may hold values from 4096 to 65535
- gain_attn: float32 [1024], replicated, may hold values from 0.5 to 1.5
- gain_latent: float32 [512], replicated, may hold values from 0.5 to 1.5
- gain_moe: float32 [1024], replicated, may hold values from 0.5 to 1.5
- w_query: bfloat16 [1024, 1024], P(None, 'ctx'), may hold values from -0.1875 to 0.1875
- w_latent: bfloat16 [1024, 512], P(None, 'ctx'), may hold values from -0.1875 to 0.1875
- w_key_up: bfloat16 [512, 1024], P(None, 'ctx'), may hold values from -0.25 to 0.25
- w_value_up: bfloat16 [512, 1024], P(None, 'ctx'), may hold values from -0.25 to 0.25
- w_out: bfloat16 [1024, 1024], P('ctx'), may hold values from -0.1875 to 0.1875
- w_gate: bfloat16 [64, 1024, 1408], P('exp', None, 'ctx'), may hold values from -0.1875 to 0.1875
- w_up: bfloat16 [64, 1024, 1408], P('exp', None, 'ctx'), may hold values from -0.1875 to 0.1875
- w_down: bfloat16 [64, 1408, 1024], P('exp', 'ctx'), may hold values from -0.15625 to 0.15625
Outputs:
- first_out: bfloat16 [8192, 1024], P('exp', 'ctx')
- second_out: bfloat16 [8192, 1024], P('exp', 'ctx')
- grad_first_out: bfloat16 [8192, 1024], P('exp', 'ctx')
- grad_second_out: bfloat16 [8192, 1024], P('exp', 'ctx')
Inputs may be any that keep to these rules, and one draw needn't show every extreme that they name: `expert_ids`: each row names 6 different experts. In each aligned block of 128 rows (one window, the rows of one index of exp) no expert is named by more than 16 rows, a bound that some expert reaches in every block.
All inputs are finite; a program needn't handle non-finite values.
Results may differ from a plain program's by a relative error of at most 0.025.
Values may be sent and summed in bfloat16 or wider, within the bound.
A program may use at most 64 MiB of HBM per device.

v0:
```python
import math
import jax
import jax.numpy as jnp
from jax import lax
from jax.sharding import PartitionSpec as P

HEAD_DIM = 128
TOP = 6
epsilon = 1e-06
soft_limit = 5.0


def rms_scale(row_data):
    return lax.rsqrt(jnp.mean(row_data * row_data, axis=-1, keepdims=True) + epsilon)


def rms_back(row_data, gain_vec, grad_in):
    factor = rms_scale(row_data)
    weighted = gain_vec * grad_in
    inner_mean = jnp.mean(weighted * row_data, axis=-1, keepdims=True)
    return factor * weighted - row_data * (factor * factor * factor) * inner_mean


def route_slots(expert_rows, expert_count):
    flat_ids = expert_rows.reshape(-1)
    labels = jnp.arange(expert_count)
    onehot = (flat_ids[:, None] == labels[None, :]).astype(jnp.int32)
    before = jnp.cumsum(onehot, axis=0) - onehot
    return jnp.sum(before * onehot, axis=1).reshape(expert_rows.shape)


def local(
    y_first,
    y_second,
    grad_first,
    grad_second,
    expert_ids,
    gate_fixed,
    gain_attn,
    gain_latent,
    gain_moe,
    w_query,
    w_latent,
    w_key_up,
    w_value_up,
    w_out,
    w_gate,
    w_up,
    w_down,
):
    ctx_count = lax.axis_size("ctx")
    exp_count = lax.axis_size("exp")
    ctx_index = lax.axis_index("ctx")
    local_experts = w_gate.shape[0]
    expert_count = exp_count * local_experts
    window_len = y_first.shape[0]
    own_cols = y_first.shape[1]
    model_width = own_cols * ctx_count
    capacity = ctx_count * (
        (window_len * TOP * 4 + 3 * expert_count * ctx_count - 1) // (3 * expert_count * ctx_count)
    )
    full_first, full_second, full_gfirst, full_gsecond = (
        lax.all_gather(y_first, "ctx", axis=1, tiled=True),
        lax.all_gather(y_second, "ctx", axis=1, tiled=True),
        lax.all_gather(grad_first, "ctx", axis=1, tiled=True),
        lax.all_gather(grad_second, "ctx", axis=1, tiled=True),
    )
    first_in = full_first.astype(jnp.float32)
    normed = (first_in * rms_scale(first_in) * gain_moe).astype(jnp.bfloat16)
    slot_ids = route_slots(expert_ids, expert_count)
    flat_slots = (expert_ids * capacity + slot_ids).reshape(-1)
    targets = jnp.arange(expert_count * capacity)
    hits = (targets[:, None] == flat_slots[None, :]).astype(jnp.bfloat16)
    chooser = jnp.max(hits.reshape(expert_count * capacity, window_len, TOP), axis=2)
    send_rows = jnp.dot(chooser, normed, preferred_element_type=jnp.float32).astype(jnp.bfloat16)
    send_rows = send_rows.reshape(expert_count, capacity, model_width)
    send_grads = jnp.dot(chooser, full_gsecond, preferred_element_type=jnp.float32).astype(
        jnp.bfloat16
    )
    send_grads = send_grads.reshape(expert_count, capacity, model_width)
    recv_rows, recv_grads = (
        lax.all_to_all(send_rows, "exp", split_axis=0, concat_axis=0, tiled=True),
        lax.all_to_all(send_grads, "exp", split_axis=0, concat_axis=0, tiled=True),
    )
    grouped_rows = recv_rows.reshape(exp_count, local_experts, capacity, model_width)
    grouped_grads = recv_grads.reshape(exp_count, local_experts, capacity, model_width)
    gate_proj = jnp.einsum(
        "secd,edf->secf", grouped_rows, w_gate, preferred_element_type=jnp.float32
    )
    up_proj = jnp.einsum("secd,edf->secf", grouped_rows, w_up, preferred_element_type=jnp.float32)
    sigmoid_gate = jax.nn.sigmoid(gate_proj)
    hidden = (gate_proj * sigmoid_gate * up_proj).astype(jnp.bfloat16)
    part_out = jnp.einsum(
        "secf,efd->secd", hidden, w_down, preferred_element_type=jnp.float32
    ).astype(jnp.bfloat16)
    grad_hidden = jnp.einsum(
        "secd,efd->secf", grouped_grads, w_down, preferred_element_type=jnp.float32
    )
    grad_gate = (
        grad_hidden * up_proj * sigmoid_gate * (1.0 + gate_proj * (1.0 - sigmoid_gate))
    ).astype(jnp.bfloat16)
    grad_up = (grad_hidden * gate_proj * sigmoid_gate).astype(jnp.bfloat16)
    part_back = jnp.einsum("secf,edf->secd", grad_gate, w_gate, preferred_element_type=jnp.float32)
    part_back = part_back + jnp.einsum(
        "secf,edf->secd", grad_up, w_up, preferred_element_type=jnp.float32
    )
    part_back = part_back.astype(jnp.bfloat16)
    weights = gate_fixed.astype(jnp.float32) / 65536.0
    back_out, back_grads = (
        lax.all_to_all(
            part_out.reshape(expert_count, capacity, model_width),
            "exp",
            split_axis=0,
            concat_axis=0,
            tiled=True,
        ),
        lax.all_to_all(
            part_back.reshape(expert_count, capacity, model_width),
            "exp",
            split_axis=0,
            concat_axis=0,
            tiled=True,
        ),
    )
    picked_out = jnp.take(
        back_out.reshape(expert_count * capacity, model_width), flat_slots, axis=0
    )
    picked_out = picked_out.reshape(window_len, TOP, model_width).astype(jnp.float32)
    picked_grads = jnp.take(
        back_grads.reshape(expert_count * capacity, model_width), flat_slots, axis=0
    )
    picked_grads = picked_grads.reshape(window_len, TOP, model_width).astype(jnp.float32)
    moe_part = jnp.sum(weights[:, :, None] * picked_out, axis=1)
    grad_part = jnp.sum(weights[:, :, None] * picked_grads, axis=1)
    moe_out, grad_moe = (
        lax.psum(moe_part.astype(jnp.bfloat16), "ctx").astype(jnp.float32),
        lax.psum(grad_part.astype(jnp.bfloat16), "ctx").astype(jnp.float32),
    )
    second_full = (full_second.astype(jnp.float32) - moe_out).astype(jnp.bfloat16)
    total_grad = full_gfirst.astype(jnp.float32) + rms_back(first_in, gain_moe, grad_moe)
    grad_first_full = total_grad.astype(jnp.bfloat16)
    second = second_full.astype(jnp.float32)
    attn_in = (second * rms_scale(second) * gain_attn).astype(jnp.bfloat16)
    queries = jnp.dot(attn_in, w_query, preferred_element_type=jnp.float32).astype(jnp.bfloat16)
    latent_part = jnp.dot(attn_in, w_latent, preferred_element_type=jnp.float32).astype(
        jnp.bfloat16
    )
    latent = lax.all_gather(latent_part, "ctx", axis=1, tiled=True)
    latent_f = latent.astype(jnp.float32)
    latent_norm = (latent_f * rms_scale(latent_f) * gain_latent).astype(jnp.bfloat16)
    key_rows = jnp.dot(latent_norm, w_key_up, preferred_element_type=jnp.float32).astype(
        jnp.bfloat16
    )
    value_rows = jnp.dot(latent_norm, w_value_up, preferred_element_type=jnp.float32).astype(
        jnp.bfloat16
    )
    local_heads = w_query.shape[1] // HEAD_DIM
    head_shape = (window_len, local_heads, HEAD_DIM)
    query_heads = queries.reshape(head_shape)
    key_heads = key_rows.reshape(head_shape)
    value_heads = value_rows.reshape(head_shape)
    scale_factor = 1.0 / math.sqrt(HEAD_DIM)
    raw_scores = (
        jnp.einsum("qhk,shk->hqs", query_heads, key_heads, preferred_element_type=jnp.float32)
        * scale_factor
    )
    bounded = jnp.tanh(raw_scores / soft_limit)
    positions = jnp.arange(window_len)
    allowed = positions[None, :] <= positions[:, None]
    exp_scores = jnp.where(allowed[None], jnp.exp(soft_limit * bounded), 0.0)
    probs_full = exp_scores / jnp.sum(exp_scores, axis=-1, keepdims=True)
    probs_low = probs_full.astype(jnp.bfloat16)
    mixed_heads = jnp.einsum(
        "hqs,shk->qhk", probs_low, value_heads, preferred_element_type=jnp.float32
    )
    mixed_heads = mixed_heads.astype(jnp.bfloat16).reshape(window_len, local_heads * HEAD_DIM)
    attn_part = jnp.dot(mixed_heads, w_out, preferred_element_type=jnp.float32)
    attn_out = lax.psum_scatter(
        attn_part.astype(jnp.bfloat16), "ctx", scatter_dimension=1, tiled=True
    ).astype(jnp.float32)
    first_out = (y_first.astype(jnp.float32) - attn_out).astype(jnp.bfloat16)
    grad_mixed = jnp.einsum(
        "td,hd->th", grad_first_full, w_out, preferred_element_type=jnp.float32
    ).astype(jnp.bfloat16)
    grad_heads = grad_mixed.reshape(head_shape)
    grad_probs = jnp.einsum(
        "qhk,shk->hqs", grad_heads, value_heads, preferred_element_type=jnp.float32
    )
    row_delta = jnp.sum(probs_full * grad_probs, axis=-1, keepdims=True)
    grad_scores = (
        probs_full * (grad_probs - row_delta) * (1.0 - bounded * bounded) * scale_factor
    ).astype(jnp.bfloat16)
    flat_width = local_heads * HEAD_DIM
    grad_queries = jnp.einsum(
        "hqs,shk->qhk", grad_scores, key_heads, preferred_element_type=jnp.float32
    )
    grad_queries = grad_queries.astype(jnp.bfloat16).reshape(window_len, flat_width)
    grad_keys = jnp.einsum(
        "hqs,qhk->shk", grad_scores, query_heads, preferred_element_type=jnp.float32
    )
    grad_keys = grad_keys.astype(jnp.bfloat16).reshape(window_len, flat_width)
    grad_values = jnp.einsum(
        "hqs,qhk->shk", probs_low, grad_heads, preferred_element_type=jnp.float32
    )
    grad_values = grad_values.astype(jnp.bfloat16).reshape(window_len, flat_width)
    latent_grad_part = jnp.einsum(
        "th,lh->tl", grad_keys, w_key_up, preferred_element_type=jnp.float32
    )
    latent_grad_part = latent_grad_part + jnp.einsum(
        "th,lh->tl", grad_values, w_value_up, preferred_element_type=jnp.float32
    )
    grad_latent_norm = lax.psum(latent_grad_part.astype(jnp.bfloat16), "ctx").astype(jnp.float32)
    grad_latent = rms_back(latent_f, gain_latent, grad_latent_norm).astype(jnp.bfloat16)
    latent_cols = w_latent.shape[1]
    own_latent = lax.dynamic_slice_in_dim(grad_latent, ctx_index * latent_cols, latent_cols, 1)
    input_part = jnp.einsum("th,dh->td", grad_queries, w_query, preferred_element_type=jnp.float32)
    input_part = input_part + jnp.einsum(
        "tl,dl->td", own_latent, w_latent, preferred_element_type=jnp.float32
    )
    grad_attn_in = lax.psum(input_part.astype(jnp.bfloat16), "ctx").astype(jnp.float32)
    full_back = rms_back(second, gain_attn, grad_attn_in)
    own_back = lax.dynamic_slice_in_dim(full_back, ctx_index * own_cols, own_cols, 1)
    grad_second_out = (grad_second.astype(jnp.float32) + own_back).astype(jnp.bfloat16)
    second_out = lax.dynamic_slice_in_dim(second_full, ctx_index * own_cols, own_cols, 1)
    grad_first_out = lax.dynamic_slice_in_dim(grad_first_full, ctx_index * own_cols, own_cols, 1)
    return (first_out, second_out, grad_first_out, grad_second_out)


def solution(mesh):
    placed = (
        P("exp", "ctx"),
        P("exp", "ctx"),
        P("exp", "ctx"),
        P("exp", "ctx"),
        P("exp", None),
        P("exp", None),
        P(),
        P(),
        P(),
        P(None, "ctx"),
        P(None, "ctx"),
        P(None, "ctx"),
        P(None, "ctx"),
        P("ctx", None),
        P("exp", None, "ctx"),
        P("exp", None, "ctx"),
        P("exp", "ctx", None),
    )
    return jax.shard_map(
        local,
        mesh=mesh,
        in_specs=placed,
        out_specs=(P("exp", "ctx"), P("exp", "ctx"), P("exp", "ctx"), P("exp", "ctx")),
        check_vma=False,
    )
```

profile of v0, /device:TPU:2, one launch (start us, length us, event | category | flops | bytes accessed | tf_op | source)
XLA Modules:
  0.0 782.4 jit_solution(9239729217433142094)
XLA Ops:
  11.8 12.6 %all_gather.16 = bf16[128,1024]{1,0:T(8,128)(2,1)S(1)} all-gather(bf16[128,128]{1,0:T(8,128)(2,1)} %param.19), channel_id=1, replica_groups=mesh['exp'=64,'ctx'=8] {'ctx'}, dimensions={1}, use_global_device_ids=true | all-gather | bytes 294912 | tf_op jit(solution)/shard_map/all_gather | solution.py:63
  27.3 18.8 %all-to-all-start = ((bf16[64,16,1024]{2,1,0:T(8,128)(2,1)}), bf16[64,16,1024]{2,1,0:T(8,128)(2,1)S(1)}, u32[]{:S(2)}, u32[]{:S(2)}) async-start(bf16[64,16,1024]{2,1,0:T(8,128)(2,1)} %bitcast.132), calls=%async_computation | async-start | bytes 4194304 | tf_op jit(solution)/shard_map/all_to_all | solution.py:82
  46.1 11.5 %all_gather.19 = bf16[128,1024]{1,0:T(8,128)(2,1)S(1)} all-gather(bf16[128,128]{1,0:T(8,128)(2,1)S(1)} %copy-done.11), channel_id=1, replica_groups=mesh['exp'=64,'ctx'=8] {'ctx'}, dimensions={1}, use_global_device_ids=true | all-gather | bytes 294912 | tf_op jit(solution)/shard_map/all_gather | solution.py:66
  59.6 82.4 %all-to-all-done = bf16[64,16,1024]{2,1,0:T(8,128)(2,1)S(1)} async-done(((bf16[64,16,1024]{2,1,0:T(8,128)(2,1)}), bf16[64,16,1024]{2,1,0:T(8,128)(2,1)S(1)}, u32[]{:S(2)}, u32[]{:S(2)}) %all-to-all-start) | async-done | bytes 2097184 | tf_op jit(solution)/shard_map/all_to_all | solution.py:82
  142.0 10.3 %all-to-all-start.2 = ((bf16[64,16,1024]{2,1,0:T(8,128)(2,1)}), bf16[64,16,1024]{2,1,0:T(8,128)(2,1)}, u32[]{:S(2)}, u32[]{:S(2)}) async-start(bf16[64,16,1024]{2,1,0:T(8,128)(2,1)} %bitcast.131), calls=%async_computation.2 | async-start | bytes 4194304 | tf_op jit(solution)/shard_map/all_to_all | solution.py:83
  155.1 94.1 %all-to-all-done.2 = bf16[64,16,1024]{2,1,0:T(8,128)(2,1)} async-done(((bf16[64,16,1024]{2,1,0:T(8,128)(2,1)}), bf16[64,16,1024]{2,1,0:T(8,128)(2,1)}, u32[]{:S(2)}, u32[]{:S(2)}) %all-to-all-start.2) | async-done | bytes 2097184 | tf_op jit(solution)/shard_map/all_to_all | solution.py:83
  249.2 2.3 convolution_bitcast_fusion
  254.7 8.8 %all-to-all-start.3 = ((bf16[64,16,1024]{2,1,0:T(8,128)(2,1)}), bf16[64,16,1024]{2,1,0:T(8,128)(2,1)S(1)}, u32[]{:S(2)}, u32[]{:S(2)}) async-start(bf16[64,16,1024]{2,1,0:T(8,128)(2,1)} %add_convert_fusion), calls=%async_computation.3 | async-start | bytes 4194304 | tf_op jit(solution)/shard_map/all_to_all | solution.py:117
  263.5 3.4 convolution_convert_fusion
  266.9 93.6 %all-to-all-done.3 = bf16[64,16,1024]{2,1,0:T(8,128)(2,1)S(1)} async-done(((bf16[64,16,1024]{2,1,0:T(8,128)(2,1)}), bf16[64,16,1024]{2,1,0:T(8,128)(2,1)S(1)}, u32[]{:S(2)}, u32[]{:S(2)}) %all-to-all-start.3) | async-done | bytes 2097184 | tf_op jit(solution)/shard_map/all_to_all | solution.py:117
  360.5 8.9 %all-to-all-start.1 = ((bf16[64,16,1024]{2,1,0:T(8,128)(2,1)}), bf16[64,16,1024]{2,1,0:T(8,128)(2,1)}, u32[]{:S(2)}, u32[]{:S(2)}) async-start(bf16[64,16,1024]{2,1,0:T(8,128)(2,1)} %convolution_convert_fusion), calls=%async_computation.1 | async-start | bytes 4194304 | tf_op jit(solution)/shard_map/all_to_all | solution.py:110
  370.7 3.6 gather_fusion.1
  374.3 92.0 %all-to-all-done.1 = bf16[64,16,1024]{2,1,0:T(8,128)(2,1)} async-done(((bf16[64,16,1024]{2,1,0:T(8,128)(2,1)}), bf16[64,16,1024]{2,1,0:T(8,128)(2,1)}, u32[]{:S(2)}, u32[]{:S(2)}) %all-to-all-start.1) | async-done | bytes 2097184 | tf_op jit(solution)/shard_map/all_to_all | solution.py:110
  466.3 6.4 gather_fusion
  472.7 4.0 select_convert_fusion.1
  476.7 4.6 reshape.255
  483.5 7.5 multiply_reduce_fusion
  491.2 11.6 %all_gather.18 = bf16[128,1024]{1,0:T(8,128)(2,1)S(1)} all-gather(bf16[128,128]{1,0:T(8,128)(2,1)S(1)} %copy-done.15), channel_id=1, replica_groups=mesh['exp'=64,'ctx'=8] {'ctx'}, dimensions={1}, use_global_device_ids=true | all-gather | bytes 294912 | tf_op jit(solution)/shard_map/all_gather | solution.py:65
  502.8 12.2 %all_gather.15 = bf16[128,1024]{1,0:T(8,128)(2,1)S(1)} all-gather(bf16[128,128]{1,0:T(8,128)(2,1)S(1)} %copy-done.16), channel_id=1, replica_groups=mesh['exp'=64,'ctx'=8] {'ctx'}, dimensions={1}, use_global_device_ids=true | all-gather | bytes 294912 | tf_op jit(solution)/shard_map/all_gather | solution.py:64
  515.0 45.9 %all-reduce.9.cloned.1.call-done = (bf16[128,1024]{1,0:T(8,128)(2,1)}, bf16[128,1024]{1,0:T(8,128)(2,1)}) async-done(((bf16[128,1024]{1,0:T(8,128)(2,1)}, bf16[128,1024]{1,0:T(8,128)(2,1)}), (bf16[128,1024]{1,0:T(8,128)(2,1)}, bf16[128,1024]{1,0:T(8,128)(2,1)})) %all-reduce.9.cloned.1.call-update) | async-done | bytes 524304 | tf_op jit(solution)/shard_map/psum | solution.py:136
  564.1 12.8 %all_gather.17 = bf16[128,512]{0,1:T(8,128)(2,1)S(1)} all-gather(bf16[128,64]{0,1:T(8,128)(2,1)S(1)} %convolution_convert_fusion.12), channel_id=1, replica_groups=mesh['exp'=64,'ctx'=8] {'ctx'}, dimensions={1}, use_global_device_ids=true | all-gather | bytes 147456 | tf_op jit(solution)/shard_map/all_gather | solution.py:148
  582.6 74.2 %all-reduce.5.cloned.1.call-done = bf16[128,512]{0,1:T(8,128)(2,1)} async-done(((bf16[128,512]{0,1:T(8,128)(2,1)}), bf16[128,512]{0,1:T(8,128)(2,1)}) %all-reduce.5.cloned.1.call-update) | async-done | bytes 131088 | tf_op jit(solution)/shard_map/psum | solution.py:212
  661.6 72.4 %all-reduce.7.cloned.1.call-done = bf16[128,1024]{1,0:T(8,128)(2,1)} async-done(((bf16[128,1024]{1,0:T(8,128)(2,1)}), bf16[128,1024]{1,0:T(8,128)(2,1)}) %all-reduce.7.cloned.1.call-update) | async-done | bytes 262160 | tf_op jit(solution)/shard_map/psum | solution.py:220
  735.9 38.4 %reduce-scatter.4.cloned.1.call-done = bf16[128,128]{1,0:T(8,128)(2,1)} async-done(((bf16[1024,128]{1,0:T(8,128)(2,1)}), bf16[128,128]{1,0:T(8,128)(2,1)}) %reduce-scatter.4.cloned.1.call-update) | async-done | bytes 32784
  (122 shorter events, 35.7 us)
Async XLA Ops:
  7.2 145.2 %copy-start = (bf16[1,1024,176]{1,2,0:T(8,128)(2,1)S(1)}, bf16[1,1024,176]{1,2,0:T(8,128)(2,1)}, u32[]{:S(2)}) copy-start(bf16[1,1024,176]{1,2,0:T(8,128)(2,1)} %param.33) | copy-start | bytes 1081348
  27.3 18.8 %copy-start.11 = (bf16[128,128]{1,0:T(8,128)(2,1)S(1)}, bf16[128,128]{1,0:T(8,128)(2,1)}, u32[]{:S(2)}) copy-start(bf16[128,128]{1,0:T(8,128)(2,1)} %param.22) | copy-start | bytes 98308
  27.3 114.7 %all-to-all-start = ((bf16[64,16,1024]{2,1,0:T(8,128)(2,1)}), bf16[64,16,1024]{2,1,0:T(8,128)(2,1)S(1)}, u32[]{:S(2)}, u32[]{:S(2)}) async-start(bf16[64,16,1024]{2,1,0:T(8,128)(2,1)} %bitcast.132), calls=%async_computation | async-start | bytes 4194304 | tf_op jit(solution)/shard_map/all_to_all | solution.py:82
  142.0 107.1 %all-to-all-start.2 = ((bf16[64,16,1024]{2,1,0:T(8,128)(2,1)}), bf16[64,16,1024]{2,1,0:T(8,128)(2,1)}, u32[]{:S(2)}, u32[]{:S(2)}) async-start(bf16[64,16,1024]{2,1,0:T(8,128)(2,1)} %bitcast.131), calls=%async_computation.2 | async-start | bytes 4194304 | tf_op jit(solution)/shard_map/all_to_all | solution.py:83
  155.1 96.4 %copy-start.3 = (f32[64,1,16,176]{3,2,0,1:T(8,128)S(1)}, f32[64,1,16,176]{3,2,0,1:T(8,128)}, u32[]{:S(2)}) copy-start(f32[64,1,16,176]{3,2,0,1:T(8,128)} %convolution_bitcast_fusion.1) | copy-start | bytes 2162692
  254.7 105.8 %all-to-all-start.3 = ((bf16[64,16,1024]{2,1,0:T(8,128)(2,1)}), bf16[64,16,1024]{2,1,0:T(8,128)(2,1)S(1)}, u32[]{:S(2)}, u32[]{:S(2)}) async-start(bf16[64,16,1024]{2,1,0:T(8,128)(2,1)} %add_convert_fusion), calls=%async_computation.3 | async-start | bytes 4194304 | tf_op jit(solution)/shard_map/all_to_all | solution.py:117
  266.9 103.0 %copy-start.19 = (s32[128,6]{0,1:T(8,128)S(1)}, s32[128,6]{0,1:T(8,128)}, u32[]{:S(2)}) copy-start(s32[128,6]{0,1:T(8,128)} %param.24) | copy-start | bytes 9220
  360.5 105.8 %all-to-all-start.1 = ((bf16[64,16,1024]{2,1,0:T(8,128)(2,1)}), bf16[64,16,1024]{2,1,0:T(8,128)(2,1)}, u32[]{:S(2)}, u32[]{:S(2)}) async-start(bf16[64,16,1024]{2,1,0:T(8,128)(2,1)} %convolution_convert_fusion), calls=%async_computation.1 | async-start | bytes 4194304 | tf_op jit(solution)/shard_map/all_to_all | solution.py:110
  369.4 191.5 %all-reduce.9.cloned.1.call-start = ((), (), s32[]{:S(2)}) async-start(), calls=%async_computation.8 | async-start | bytes 1048576 | tf_op jit(solution)/shard_map/psum | solution.py:136
  483.5 19.3 %copy-start.16 = (bf16[128,128]{1,0:T(8,128)(2,1)S(1)}, bf16[128,128]{1,0:T(8,128)(2,1)}, u32[]{:S(2)}) copy-start(bf16[128,128]{1,0:T(8,128)(2,1)} %param.20) | copy-start | bytes 98308
  483.5 77.4 %copy-start.2 = (bf16[128,1024]{1,0:T(8,128)(2,1)S(1)}, bf16[128,1024]{1,0:T(8,128)(2,1)}, u32[]{:S(2)}) copy-start(bf16[128,1024]{1,0:T(8,128)(2,1)} %copy-done.1) | copy-start | bytes 786436
  491.0 72.7 %copy-start.10 = (bf16[1024,64]{0,1:T(8,128)(2,1)S(1)}, bf16[1024,64]{0,1:T(8,128)(2,1)}, u32[]{:S(2)}) copy-start(bf16[1024,64]{0,1:T(8,128)(2,1)} %param.29) | copy-start | bytes 393220
  491.0 72.7 %copy-start.18 = (f32[1024]{0:T(1024)S(1)}, f32[1024]{0:T(1024)}, u32[]{:S(2)}) copy-start(f32[1024]{0:T(1024)} %param.25) | copy-start | bytes 12292
  491.0 86.4 %copy-start.8 = (bf16[1024,128]{1,0:T(8,128)(2,1)S(1)}, bf16[1024,128]{1,0:T(8,128)(2,1)}, u32[]{:S(2)}) copy-start(bf16[1024,128]{1,0:T(8,128)(2,1)} %param.28) | copy-start | bytes 786436
  491.1 165.7 %all-reduce.5.cloned.1.call-start = ((), (), s32[]{:S(2)}) async-start(), calls=%async_computation.5 | async-start | bytes 262144 | tf_op jit(solution)/shard_map/psum | solution.py:212
  491.1 86.6 %copy-start.9 = (bf16[512,128]{1,0:T(8,128)(2,1)S(1)}, bf16[512,128]{1,0:T(8,128)(2,1)}, u32[]{:S(2)}) copy-start(bf16[512,128]{1,0:T(8,128)(2,1)} %param.30) | copy-start | bytes 393220
  491.1 86.6 %copy-start.20 = (f32[512]{0:T(512)S(1)}, f32[512]{0:T(512)}, u32[]{:S(2)}) copy-start(f32[512]{0:T(512)} %param.26) | copy-start | bytes 6148
  502.8 75.3 %copy-start.13 = (bf16[512,128]{1,0:T(8,128)(2,1)S(1)}, bf16[512,128]{1,0:T(8,128)(2,1)}, u32[]{:S(2)}) copy-start(bf16[512,128]{1,0:T(8,128)(2,1)} %param.31) | copy-start | bytes 393220
  579.2 78.6 %copy-start.25 = (f32[128]{0:T(128)S(1)}, f32[128]{0:T(128)}, u32[]{:S(2)}) copy-start(f32[128]{0:T(128)} %get-tuple-element.19) | copy-start | bytes 1540
  582.0 152.0 %all-reduce.7.cloned.1.call-start = ((), (), s32[]{:S(2)}) async-start(), calls=%async_computation.6 | async-start | bytes 524288 | tf_op jit(solution)/shard_map/psum | solution.py:220
  582.5 152.7 %copy-start.22 = (f32[128]{0:T(128)S(1)}, f32[128]{0:T(128)}, u32[]{:S(2)}) copy-start(f32[128]{0:T(128)} %get-tuple-element.17) | copy-start | bytes 1540
  582.5 152.7 %copy-start.24 = (f32[128]{0:T(128)S(1)}, f32[128]{0:T(128)}, u32[]{:S(2)}) copy-start(f32[128]{0:T(128)} %copy-done.23) | copy-start | bytes 1540
  582.6 192.6 %copy-start.12 = (bf16[128,128]{1,0:T(8,128)(2,1)S(1)}, bf16[128,128]{1,0:T(8,128)(2,1)}, u32[]{:S(2)}) copy-start(bf16[128,128]{1,0:T(8,128)(2,1)} %param.19) | copy-start | bytes 98308
  659.5 114.8 %reduce-scatter.4.cloned.1.call-start = ((), (), s32[]{:S(2)}) async-start(), calls=%async_computation.7 | async-start | bytes 294912
  (11 other events, 96.3 us)
Sparse Core Ops, SparseCore 0:
  491.2 69.6 all-reduce.8
  582.1 74.5 all-reduce.4
  659.6 74.4 all-reduce.6
  736.9 37.3 reduce-scatter.3
where the time goes:
time: 783 us; the launch traced here: 782 us
  waiting for transfers between devices  593 us (76%)
  blocking collectives  60.7 us (8%)
  starting transfers between devices  47.2 us (6%)
  local copies, waits for them, and re-layouts  22.7 us (3%)
  other arithmetic  22.6 us (3%)
  matrix products  21.9 us (3%)
  between operations  14.2 us (2%)
    all_to_all x1, waiting for transfers between devices, local(): lax.all_to_all(send_grads, 'exp', split_axis=0, concat_axis=0, tiled=True)  94.1 us
    all_to_all x1, waiting for transfers between devices, local(): lax.all_to_all(part_back.reshape(expert_count, capacity, model_width), 'e...  93.6 us
    all_to_all x1, waiting for transfers between devices, local(): lax.all_to_all(part_out.reshape(expert_count, capacity, model_width), 'ex...  92 us
    all_to_all x1, waiting for transfers between devices, local(): lax.all_to_all(send_rows, 'exp', split_axis=0, concat_axis=0, tiled=True)  82.4 us
    psum x1, waiting for transfers between devices, local(): lax.psum(latent_grad_part.astype(jnp.bfloat16), 'ctx').astype(jnp.float32)  74.2 us
    psum x1, waiting for transfers between devices, local(): lax.psum(input_part.astype(jnp.bfloat16), 'ctx').astype(jnp.float32)  72.4 us
    psum x1, waiting for transfers between devices, local(): lax.psum(moe_part.astype(jnp.bfloat16), 'ctx').astype(jnp.float32)  45.9 us
    unnamed x5, waiting for transfers between devices  38.4 us
  transfers between devices with their start and end apart: 8, of which 8 were waited for; matrix products, arithmetic and copies ran while one was open for 2% of the time, Pallas kernels for 0%

commit v1 on v0

--- a/solution.py
+++ b/solution.py
@@ -8,6 +8,11 @@
 TOP = 6
 epsilon = 1e-06
 soft_limit = 5.0
+
+
+def sheet_group(base_x):
+    block_out = lax.all_gather(base_x, "ctx").sum(axis=0)
+    return block_out
 
 
 def rms_scale(row_data):
@@ -133,7 +138,7 @@
     moe_part = jnp.sum(weights[:, :, None] * picked_out, axis=1)
     grad_part = jnp.sum(weights[:, :, None] * picked_grads, axis=1)
     moe_out, grad_moe = (
-        lax.psum(moe_part.astype(jnp.bfloat16), "ctx").astype(jnp.float32),
+        sheet_group(moe_part.astype(jnp.bfloat16)).astype(jnp.float32),
         lax.psum(grad_part.astype(jnp.bfloat16), "ctx").astype(jnp.float32),
     )
     second_full = (full_second.astype(jnp.float32) - moe_out).astype(jnp.bfloat16)

time: 783 us -> 814 us (1.040)
  waiting for transfers between devices: 593 us -> 624 us
    all_gather x0 -> x1, waiting for transfers between devices: none -> 31.2 us  [sheet_group(): block_out = lax.all_gather(base_x, 'ctx').sum(axis=0)]
    unnamed x5 -> x6, waiting for transfers between devices: 38.4 us -> 39.2 us
  transfers between devices with their start and end apart: 8 -> 9, of which waited for: 8 -> 9; matrix products, arithmetic and copies ran while one was open for 2% -> 2% of each run, Pallas kernels for 0% -> 0%
where the time goes in v1:
time: 814 us; the launch traced here: 813 us
  waiting for transfers between devices  624 us (77%)
  blocking collectives  60.1 us (7%)
  starting transfers between devices  47.2 us (6%)
  local copies, waits for them, and re-layouts  23.2 us (3%)
  other arithmetic  23 us (3%)
  matrix products  20.5 us (3%)
  between operations  14.2 us (2%)
    all_to_all x1, waiting for transfers between devices, local(): lax.all_to_all(send_grads, 'exp', split_axis=0, concat_axis=0, tiled=True)  94.1 us
    all_to_all x1, waiting for transfers between devices, local(): lax.all_to_all(part_back.reshape(expert_count, capacity, model_width), 'e...  93.6 us
    all_to_all x1, waiting for transfers between devices, local(): lax.all_to_all(part_out.reshape(expert_count, capacity, model_width), 'ex...  92 us
    all_to_all x1, waiting for transfers between devices, local(): lax.all_to_all(send_rows, 'exp', split_axis=0, concat_axis=0, tiled=True)  82.4 us
    psum x1, waiting for transfers between devices, local(): lax.psum(latent_grad_part.astype(jnp.bfloat16), 'ctx').astype(jnp.float32)  74.5 us
    psum x1, waiting for transfers between devices, local(): lax.psum(input_part.astype(jnp.bfloat16), 'ctx').astype(jnp.float32)  72.6 us
    psum x1, waiting for transfers between devices, local(): lax.psum(grad_part.astype(jnp.bfloat16), 'ctx').astype(jnp.float32)  44.9 us
    unnamed x6, waiting for transfers between devices  39.2 us
  transfers between devices with their start and end apart: 9, of which 9 were waited for; matrix products, arithmetic and copies ran while one was open for 2% of the time, Pallas kernels for 0%

profile of v1, /device:TPU:2, one launch (start us, length us, event | category | flops | bytes accessed | tf_op | source)
XLA Modules:
  0.0 812.5 jit_solution(13778810139765253252)
XLA Ops:
  11.8 12.6 %all_gather.20 = bf16[128,1024]{1,0:T(8,128)(2,1)S(1)} all-gather(bf16[128,128]{1,0:T(8,128)(2,1)} %param.19), channel_id=1, replica_groups=mesh['exp'=64,'ctx'=8] {'ctx'}, dimensions={1}, use_global_device_ids=true | all-gather | bytes 294912 | tf_op jit(solution)/shard_map/all_gather | solution.py:68
  27.3 18.8 %all-to-all-start = ((bf16[64,16,1024]{2,1,0:T(8,128)(2,1)}), bf16[64,16,1024]{2,1,0:T(8,128)(2,1)S(1)}, u32[]{:S(2)}, u32[]{:S(2)}) async-start(bf16[64,16,1024]{2,1,0:T(8,128)(2,1)} %bitcast.133), calls=%async_computation | async-start | bytes 4194304 | tf_op jit(solution)/shard_map/all_to_all | solution.py:87
  46.1 11.5 %all_gather.24 = bf16[128,1024]{1,0:T(8,128)(2,1)S(1)} all-gather(bf16[128,128]{1,0:T(8,128)(2,1)S(1)} %copy-done.10), channel_id=1, replica_groups=mesh['exp'=64,'ctx'=8] {'ctx'}, dimensions={1}, use_global_device_ids=true | all-gather | bytes 294912 | tf_op jit(solution)/shard_map/all_gather | solution.py:71
  59.6 82.4 %all-to-all-done = bf16[64,16,1024]{2,1,0:T(8,128)(2,1)S(1)} async-done(((bf16[64,16,1024]{2,1,0:T(8,128)(2,1)}), bf16[64,16,1024]{2,1,0:T(8,128)(2,1)S(1)}, u32[]{:S(2)}, u32[]{:S(2)}) %all-to-all-start) | async-done | bytes 2097184 | tf_op jit(solution)/shard_map/all_to_all | solution.py:87
  142.0 10.3 %all-to-all-start.2 = ((bf16[64,16,1024]{2,1,0:T(8,128)(2,1)}), bf16[64,16,1024]{2,1,0:T(8,128)(2,1)}, u32[]{:S(2)}, u32[]{:S(2)}) async-start(bf16[64,16,1024]{2,1,0:T(8,128)(2,1)} %bitcast.132), calls=%async_computation.2 | async-start | bytes 4194304 | tf_op jit(solution)/shard_map/all_to_all | solution.py:88
  155.1 94.1 %all-to-all-done.2 = bf16[64,16,1024]{2,1,0:T(8,128)(2,1)} async-done(((bf16[64,16,1024]{2,1,0:T(8,128)(2,1)}), bf16[64,16,1024]{2,1,0:T(8,128)(2,1)}, u32[]{:S(2)}, u32[]{:S(2)}) %all-to-all-start.2) | async-done | bytes 2097184 | tf_op jit(solution)/shard_map/all_to_all | solution.py:88
  254.7 8.8 %all-to-all-start.3 = ((bf16[64,16,1024]{2,1,0:T(8,128)(2,1)}), bf16[64,16,1024]{2,1,0:T(8,128)(2,1)S(1)}, u32[]{:S(2)}, u32[]{:S(2)}) async-start(bf16[64,16,1024]{2,1,0:T(8,128)(2,1)} %add_convert_fusion), calls=%async_computation.3 | async-start | bytes 4194304 | tf_op jit(solution)/shard_map/all_to_all | solution.py:122
  263.5 3.4 convolution_convert_fusion
  266.9 93.6 %all-to-all-done.3 = bf16[64,16,1024]{2,1,0:T(8,128)(2,1)S(1)} async-done(((bf16[64,16,1024]{2,1,0:T(8,128)(2,1)}), bf16[64,16,1024]{2,1,0:T(8,128)(2,1)S(1)}, u32[]{:S(2)}, u32[]{:S(2)}) %all-to-all-start.3) | async-done | bytes 2097184 | tf_op jit(solution)/shard_map/all_to_all | solution.py:122
  360.5 8.9 %all-to-all-start.1 = ((bf16[64,16,1024]{2,1,0:T(8,128)(2,1)}), bf16[64,16,1024]{2,1,0:T(8,128)(2,1)}, u32[]{:S(2)}, u32[]{:S(2)}) async-start(bf16[64,16,1024]{2,1,0:T(8,128)(2,1)} %convolution_convert_fusion), calls=%async_computation.1 | async-start | bytes 4194304 | tf_op jit(solution)/shard_map/all_to_all | solution.py:115
  370.6 3.6 gather_fusion.1
  374.2 92.0 %all-to-all-done.1 = bf16[64,16,1024]{2,1,0:T(8,128)(2,1)} async-done(((bf16[64,16,1024]{2,1,0:T(8,128)(2,1)}), bf16[64,16,1024]{2,1,0:T(8,128)(2,1)}, u32[]{:S(2)}, u32[]{:S(2)}) %all-to-all-start.1) | async-done | bytes 2097184 | tf_op jit(solution)/shard_map/all_to_all | solution.py:115
  466.3 6.4 gather_fusion
  472.7 4.0 select_convert_fusion.1
  476.7 4.6 reshape.263
  483.5 7.5 multiply_reduce_fusion
  491.8 11.5 %all_gather.23 = bf16[128,1024]{1,0:T(8,128)(2,1)S(1)} all-gather(bf16[128,128]{1,0:T(8,128)(2,1)S(1)} %copy-done.14), channel_id=1, replica_groups=mesh['exp'=64,'ctx'=8] {'ctx'}, dimensions={1}, use_global_device_ids=true | all-gather | bytes 294912 | tf_op jit(solution)/shard_map/all_gather | solution.py:70
  503.4 11.6 %all_gather.19 = bf16[128,1024]{1,0:T(8,128)(2,1)S(1)} all-gather(bf16[128,128]{1,0:T(8,128)(2,1)S(1)} %copy-done.15), channel_id=1, replica_groups=mesh['exp'=64,'ctx'=8] {'ctx'}, dimensions={1}, use_global_device_ids=true | all-gather | bytes 294912 | tf_op jit(solution)/shard_map/all_gather | solution.py:69
  515.0 44.9 %all-reduce.4.cloned.1.call-done = bf16[128,1024]{1,0:T(8,128)(2,1)} async-done(((bf16[128,1024]{1,0:T(8,128)(2,1)}), bf16[128,1024]{1,0:T(8,128)(2,1)}) %all-reduce.4.cloned.1.call-update) | async-done | bytes 262160 | tf_op jit(solution)/shard_map/psum | solution.py:142
  563.1 31.2 %all-gather.3.cloned.1.call-done = bf16[1024,1024]{1,0:T(8,128)(2,1)} async-done(((bf16[128,1024]{1,0:T(8,128)(2,1)}), bf16[1024,1024]{1,0:T(8,128)(2,1)}) %all-gather.3.cloned.1.call-update) | async-done | bytes 2097168 | tf_op jit(solution)/shard_map/all_gather | solution.py:14
  596.9 12.8 %all_gather.22 = bf16[128,512]{0,1:T(8,128)(2,1)S(1)} all-gather(bf16[128,64]{0,1:T(8,128)(2,1)S(1)} %convolution_convert_fusion.12), channel_id=1, replica_groups=mesh['exp'=64,'ctx'=8] {'ctx'}, dimensions={1}, use_global_device_ids=true | all-gather | bytes 147456 | tf_op jit(solution)/shard_map/all_gather | solution.py:153
  613.1 74.5 %all-reduce.6.cloned.1.call-done = bf16[128,512]{0,1:T(8,128)(2,1)} async-done(((bf16[128,512]{0,1:T(8,128)(2,1)}), bf16[128,512]{0,1:T(8,128)(2,1)}) %all-reduce.6.cloned.1.call-update) | async-done | bytes 131088 | tf_op jit(solution)/shard_map/psum | solution.py:217
  691.6 72.6 %all-reduce.8.cloned.1.call-done = bf16[128,1024]{1,0:T(8,128)(2,1)} async-done(((bf16[128,1024]{1,0:T(8,128)(2,1)}), bf16[128,1024]{1,0:T(8,128)(2,1)}) %all-reduce.8.cloned.1.call-update) | async-done | bytes 262160 | tf_op jit(solution)/shard_map/psum | solution.py:225
  766.1 38.4 %reduce-scatter.4.cloned.1.call-done = bf16[128,128]{1,0:T(8,128)(2,1)} async-done(((bf16[1024,128]{1,0:T(8,128)(2,1)}), bf16[128,128]{1,0:T(8,128)(2,1)}) %reduce-scatter.4.cloned.1.call-update) | async-done | bytes 32784
  (110 shorter events, 38.3 us)
Async XLA Ops:
  7.2 145.2 %copy-start = (bf16[1,1024,176]{1,2,0:T(8,128)(2,1)S(1)}, bf16[1,1024,176]{1,2,0:T(8,128)(2,1)}, u32[]{:S(2)}) copy-start(bf16[1,1024,176]{1,2,0:T(8,128)(2,1)} %param.33) | copy-start | bytes 1081348
  7.2 18.0 %copy-start.13 = (f32[1024]{0:T(1024)S(1)}, f32[1024]{0:T(1024)}, u32[]{:S(2)}) copy-start(f32[1024]{0:T(1024)} %param.27) | copy-start | bytes 12292
  27.3 18.8 %copy-start.10 = (bf16[128,128]{1,0:T(8,128)(2,1)S(1)}, bf16[128,128]{1,0:T(8,128)(2,1)}, u32[]{:S(2)}) copy-start(bf16[128,128]{1,0:T(8,128)(2,1)} %param.22) | copy-start | bytes 98308
  27.3 114.7 %all-to-all-start = ((bf16[64,16,1024]{2,1,0:T(8,128)(2,1)}), bf16[64,16,1024]{2,1,0:T(8,128)(2,1)S(1)}, u32[]{:S(2)}, u32[]{:S(2)}) async-start(bf16[64,16,1024]{2,1,0:T(8,128)(2,1)} %bitcast.133), calls=%async_computation | async-start | bytes 4194304 | tf_op jit(solution)/shard_map/all_to_all | solution.py:87
  142.0 107.1 %all-to-all-start.2 = ((bf16[64,16,1024]{2,1,0:T(8,128)(2,1)}), bf16[64,16,1024]{2,1,0:T(8,128)(2,1)}, u32[]{:S(2)}, u32[]{:S(2)}) async-start(bf16[64,16,1024]{2,1,0:T(8,128)(2,1)} %bitcast.132), calls=%async_computation.2 | async-start | bytes 4194304 | tf_op jit(solution)/shard_map/all_to_all | solution.py:88
  155.1 96.5 %copy-start.3 = (f32[64,1,16,176]{3,2,0,1:T(8,128)S(1)}, f32[64,1,16,176]{3,2,0,1:T(8,128)}, u32[]{:S(2)}) copy-start(f32[64,1,16,176]{3,2,0,1:T(8,128)} %convolution_bitcast_fusion.1) | copy-start | bytes 2162692
  254.7 105.8 %all-to-all-start.3 = ((bf16[64,16,1024]{2,1,0:T(8,128)(2,1)}), bf16[64,16,1024]{2,1,0:T(8,128)(2,1)S(1)}, u32[]{:S(2)}, u32[]{:S(2)}) async-start(bf16[64,16,1024]{2,1,0:T(8,128)(2,1)} %add_convert_fusion), calls=%async_computation.3 | async-start | bytes 4194304 | tf_op jit(solution)/shard_map/all_to_all | solution.py:122
  266.9 102.9 %copy-start.17 = (s32[128,6]{0,1:T(8,128)S(1)}, s32[128,6]{0,1:T(8,128)}, u32[]{:S(2)}) copy-start(s32[128,6]{0,1:T(8,128)} %param.24) | copy-start | bytes 9220
  360.5 105.8 %all-to-all-start.1 = ((bf16[64,16,1024]{2,1,0:T(8,128)(2,1)}), bf16[64,16,1024]{2,1,0:T(8,128)(2,1)}, u32[]{:S(2)}, u32[]{:S(2)}) async-start(bf16[64,16,1024]{2,1,0:T(8,128)(2,1)} %convolution_convert_fusion), calls=%async_computation.1 | async-start | bytes 4194304 | tf_op jit(solution)/shard_map/all_to_all | solution.py:115
  369.4 190.5 %all-reduce.4.cloned.1.call-start = ((), (), s32[]{:S(2)}) async-start(), calls=%async_computation.5 | async-start | bytes 524288 | tf_op jit(solution)/shard_map/psum | solution.py:142
  483.5 19.9 %copy-start.15 = (bf16[128,128]{1,0:T(8,128)(2,1)S(1)}, bf16[128,128]{1,0:T(8,128)(2,1)}, u32[]{:S(2)}) copy-start(bf16[128,128]{1,0:T(8,128)(2,1)} %param.20) | copy-start | bytes 98308
  483.5 76.4 %copy-start.2 = (bf16[128,1024]{1,0:T(8,128)(2,1)S(1)}, bf16[128,1024]{1,0:T(8,128)(2,1)}, u32[]{:S(2)}) copy-start(bf16[128,1024]{1,0:T(8,128)(2,1)} %copy-done.1) | copy-start | bytes 786436
  491.0 71.8 %copy-start.6 = (bf16[128,1024]{1,0:T(8,128)(2,1)S(1)}, bf16[128,1024]{1,0:T(8,128)(2,1)}, u32[]{:S(2)}) copy-start(bf16[128,1024]{1,0:T(8,128)(2,1)} %param.32) | copy-start | bytes 786436
  491.0 103.3 %all-gather.3.cloned.1.call-start = ((), (), s32[]{:S(2)}) async-start(), calls=%async_computation.8 | async-start | bytes 2359296 | tf_op jit(solution)/shard_map/all_gather | solution.py:14
  491.8 195.8 %all-reduce.6.cloned.1.call-start = ((), (), s32[]{:S(2)}) async-start(), calls=%async_computation.6 | async-start | bytes 262144 | tf_op jit(solution)/shard_map/psum | solution.py:217
  563.0 33.5 %copy-start.9 = (bf16[1024,64]{0,1:T(8,128)(2,1)S(1)}, bf16[1024,64]{0,1:T(8,128)(2,1)}, u32[]{:S(2)}) copy-start(bf16[1024,64]{0,1:T(8,128)(2,1)} %param.29) | copy-start | bytes 393220
  563.1 33.5 %copy-start.16 = (f32[1024]{0:T(1024)S(1)}, f32[1024]{0:T(1024)}, u32[]{:S(2)}) copy-start(f32[1024]{0:T(1024)} %param.25) | copy-start | bytes 12292
  594.3 15.4 %copy-start.7 = (bf16[1024,128]{1,0:T(8,128)(2,1)S(1)}, bf16[1024,128]{1,0:T(8,128)(2,1)}, u32[]{:S(2)}) copy-start(bf16[1024,128]{1,0:T(8,128)(2,1)} %param.28) | copy-start | bytes 786436
  596.3 13.7 %copy-start.8 = (bf16[512,128]{1,0:T(8,128)(2,1)S(1)}, bf16[512,128]{1,0:T(8,128)(2,1)}, u32[]{:S(2)}) copy-start(bf16[512,128]{1,0:T(8,128)(2,1)} %param.30) | copy-start | bytes 393220
  596.3 13.7 %copy-start.18 = (f32[512]{0:T(512)S(1)}, f32[512]{0:T(512)}, u32[]{:S(2)}) copy-start(f32[512]{0:T(512)} %param.26) | copy-start | bytes 6148
  596.3 14.1 %copy-start.12 = (bf16[512,128]{1,0:T(8,128)(2,1)S(1)}, bf16[512,128]{1,0:T(8,128)(2,1)}, u32[]{:S(2)}) copy-start(bf16[512,128]{1,0:T(8,128)(2,1)} %param.31) | copy-start | bytes 393220
  612.6 151.6 %all-reduce.8.cloned.1.call-start = ((), (), s32[]{:S(2)}) async-start(), calls=%async_computation.7 | async-start | bytes 524288 | tf_op jit(solution)/shard_map/psum | solution.py:225
  688.7 116.7 %copy-start.11 = (bf16[128,128]{1,0:T(8,128)(2,1)S(1)}, bf16[128,128]{1,0:T(8,128)(2,1)}, u32[]{:S(2)}) copy-start(bf16[128,128]{1,0:T(8,128)(2,1)} %param.19) | copy-start | bytes 98308
  689.7 114.8 %reduce-scatter.4.cloned.1.call-start = ((), (), s32[]{:S(2)}) async-start(), calls=%async_computation.9 | async-start | bytes 294912
  (4 other events, 11.1 us)
Sparse Core Ops, SparseCore 0:
  491.2 68.6 all-reduce.3
  562.2 32.0 all-gather.2
  612.7 74.8 all-reduce.5
  689.8 74.4 all-reduce.7
  767.1 37.3 reduce-scatter.3
